TPU v7x, 256 devices: a whole 4x4x8 slice. The times are simulated.
256 devices in a mesh: dp: 4 (over y_hi, core), seq: 64 (over y_lo, x, z).
Axes of the slice: x: 4, y: 4 (y_hi: 2, y_lo: 2; y = y_hi * 2 + y_lo), z: 8, core: 2. Of those that a mesh axis runs over, the one named last changes fastest.
Arguments:
- inputs: bfloat16 [4096, 8, 1536], P('seq', 'dp'), may hold values from -6 to 6
- query_proj: bfloat16 [4096, 8, 1536], P('seq', 'dp'), may hold values from -8 to 8
- key_proj: bfloat16 [4096, 8, 1536], P('seq', 'dp'), may hold values from -8 to 8
- value_proj: bfloat16 [4096, 8, 1536], P('seq', 'dp'), may hold values from -6 to 6
- lengths: int32 [8], P('dp'), may hold values from 1024 to 4096, as said below
- out_weight: bfloat16 [1536, 1536], P('dp'), may hold values from -0.15625 to 0.15625
- norm_gain: float32 [1536], replicated, may hold values from 0.25 to 1.75
- conv_weight: float32 [31, 1536], replicated, may hold values from -1 to 1
- cotangent: bfloat16 [4096, 8, 1536], P('seq', 'dp'), may hold values from -6 to 6
Outputs:
- block_out: bfloat16 [4096, 8, 1536], P('seq', 'dp')
- grad_input: bfloat16 [4096, 8, 1536], P('seq', 'dp')
- grad_query: bfloat16 [4096, 8, 1536], P('seq', 'dp')
- grad_key: bfloat16 [4096, 8, 1536], P('seq', 'dp')
- grad_value: bfloat16 [4096, 8, 1536], P('seq', 'dp')
- grad_weight: float32 [1536, 1536], P('dp')
- grad_gain: float32 [1536], replicated
- grad_conv: float32 [31, 1536], replicated
Inputs may be any that keep to these rules, and one draw needn't show every extreme that they name: `lengths`: some utterance has all 4096 frames valid in every draw.
All inputs are finite; a program needn't handle non-finite values.
Results may differ from a plain program's by a relative error of at most 0.028.
Values may be sent and summed in bfloat16 or wider, within the bound.
No kernel may reach another device: no remote copies, remote signals or barrier semaphores. Data moves between devices by JAX's collectives and lax.ppermute only.
A program may use at most 128 MiB of HBM per device.

v0:
```python
import math

import jax
import jax.numpy as jnp
from jax import lax
from jax.sharding import PartitionSpec as P

H = 16


EPSILON = 1e-05


def with_halo(shard, sides, width):
    for axis, dim in sides:
        count, length = (lax.axis_size(axis), shard.shape[dim])
        up = [(i, (i + 1) % count) for i in range(count - 1)]
        down = [(j, i) for i, j in up]
        last = lax.slice_in_dim(shard, length - width, length, axis=dim)
        leading = lax.slice_in_dim(shard, 0, width, axis=dim)
        before = lax.ppermute(last, axis, up)
        after = lax.ppermute(leading, axis, down)
        shard = jnp.concatenate([before, shard, after], axis=dim)
    return shard


def block_size():
    return 512


def forward_item(query_item, key_item, value_item, valid_count):
    query_rows, head_width = query_item.shape
    score_scale = 1.0 / math.sqrt(head_width)
    key_valid = jnp.arange(key_item.shape[0]) < valid_count
    block_rows = block_size()

    def one_block(query_block):
        scores = (
            jnp.einsum("qd,kd->qk", query_block, key_item, preferred_element_type=jnp.float32)
            * score_scale
        )
        scores = jnp.where(key_valid[None, :], scores, -jnp.inf)
        highest = jnp.max(scores, axis=-1, keepdims=True)
        powers = jnp.exp(scores - highest)
        totals = jnp.sum(powers, axis=-1, keepdims=True)
        probs_low = (powers / totals).astype(jnp.bfloat16)
        mixed = jnp.dot(probs_low, value_item, preferred_element_type=jnp.float32).astype(
            jnp.bfloat16
        )
        return (mixed, highest[:, 0] + jnp.log(totals[:, 0]))

    mixed, log_total = lax.map(
        one_block, query_item.reshape(query_rows // block_rows, block_rows, head_width)
    )
    return (mixed.reshape(query_rows, head_width), log_total.reshape(query_rows))


def backward_item(query_item, key_item, value_item, valid_count, log_total, grad_mixed):
    query_rows, head_width = query_item.shape
    score_scale = 1.0 / math.sqrt(head_width)
    key_valid = jnp.arange(key_item.shape[0]) < valid_count
    block_rows = block_size()
    block_count = query_rows // block_rows

    def block_step(totals_pair, packed):
        key_total, value_total = totals_pair
        query_block, total_block, grad_block = packed
        scores = (
            jnp.einsum("qd,kd->qk", query_block, key_item, preferred_element_type=jnp.float32)
            * score_scale
        )
        scores = jnp.where(key_valid[None, :], scores, -jnp.inf)
        probs = jnp.exp(scores - total_block[:, None])
        probs_low = probs.astype(jnp.bfloat16)
        value_total = value_total + jnp.einsum(
            "qk,qd->kd", probs_low, grad_block, preferred_element_type=jnp.float32
        )
        grad_probs = jnp.einsum(
            "qd,kd->qk", grad_block, value_item, preferred_element_type=jnp.float32
        )
        centre = jnp.sum(probs * grad_probs, axis=-1, keepdims=True)
        grad_scores = (probs * (grad_probs - centre) * score_scale).astype(jnp.bfloat16)
        grad_query = jnp.dot(grad_scores, key_item, preferred_element_type=jnp.float32).astype(
            jnp.bfloat16
        )
        key_total = key_total + jnp.einsum(
            "qk,qd->kd", grad_scores, query_block, preferred_element_type=jnp.float32
        )
        return ((key_total, value_total), grad_query)

    zero_start = jnp.zeros(key_item.shape, jnp.float32)
    packed_blocks = (
        query_item.reshape(block_count, block_rows, head_width),
        log_total.reshape(block_count, block_rows),
        grad_mixed.reshape(block_count, block_rows, head_width),
    )
    (key_total, value_total), grad_query = lax.scan(
        block_step, (zero_start, zero_start), packed_blocks
    )
    return (grad_query.reshape(query_rows, head_width), key_total, value_total)


def run_forward(packed):
    return forward_item(packed[0], packed[1], packed[2], packed[3])


def run_backward(packed):
    return backward_item(packed[0], packed[1], packed[2], packed[3], packed[4], packed[5])


def per_device(
    inputs, query_proj, key_proj, value_proj, lengths, out_weight, norm_gain, conv_weight, cotangent
):
    frames, utterances, width = inputs.shape
    groups = lax.axis_size("seq")
    head_width = width // H
    pair_count = utterances * H
    item_count = max(1, pair_count // groups)
    query_split = max(1, groups // pair_count)
    group_count = pair_count // item_count
    sub_rows = frames // query_split
    row_count = frames * utterances
    kernel_taps = conv_weight.shape[0]
    rim_width = (kernel_taps - 1) // 2
    position = lax.axis_index("seq") * frames + jnp.arange(frames)
    keep_mask = (position[:, None] < lengths[None, :]).astype(jnp.float32)[:, :, None]
    item_ids = lax.axis_index("seq") // query_split * item_count + jnp.arange(item_count)
    owner_pick = (item_ids // H)[:, None] == jnp.arange(utterances)[None, :]
    item_lengths = jnp.sum(jnp.where(owner_pick, lengths[None, :], 0), axis=1)

    def query_send(tensor):
        shaped = tensor.reshape(query_split, sub_rows, group_count, item_count, head_width)
        return shaped.transpose(2, 0, 1, 3, 4).reshape(groups, sub_rows, item_count, head_width)

    def whole_send(tensor):
        shaped = tensor.reshape(frames, group_count, item_count, head_width).transpose(1, 0, 2, 3)
        copies = jnp.broadcast_to(
            shaped[:, None], (group_count, query_split, frames, item_count, head_width)
        )
        return copies.reshape(groups, frames, item_count, head_width)

    def to_items(tensor):
        return tensor.reshape(-1, item_count, head_width).transpose(1, 0, 2)

    def rows_send(tensor):
        return tensor.transpose(1, 0, 2).reshape(groups, -1, item_count, head_width)

    def query_back(tensor):
        shaped = tensor.reshape(group_count, query_split, sub_rows, item_count, head_width)
        return shaped.transpose(1, 2, 0, 3, 4).reshape(frames, utterances, width)

    def whole_back(tensor):
        shaped = tensor.reshape(group_count, query_split, frames, item_count, head_width)
        return jnp.sum(shaped, axis=1).transpose(1, 0, 2, 3).reshape(frames, utterances, width)

    def to_frames(tensor):
        return tensor.reshape(frames, utterances, width)

    head_query = lax.all_to_all(
        query_send(query_proj), "seq", split_axis=0, concat_axis=0, tiled=True
    )
    head_key, head_value = (
        lax.all_to_all(whole_send(key_proj), "seq", split_axis=0, concat_axis=0, tiled=True),
        lax.all_to_all(whole_send(value_proj), "seq", split_axis=0, concat_axis=0, tiled=True),
    )
    query_items = to_items(head_query)
    key_items = to_items(head_key)
    value_items = to_items(head_value)
    mixed_items, log_totals = lax.map(
        run_forward, (query_items, key_items, value_items, item_lengths)
    )
    attention = query_back(
        lax.all_to_all(rows_send(mixed_items), "seq", split_axis=0, concat_axis=0, tiled=True)
    )
    flat_attn = attention.reshape(row_count, width)
    columns = flat_attn
    projected = jnp.dot(
        columns,
        lax.all_gather(out_weight, "dp", axis=0, tiled=True),
        preferred_element_type=jnp.float32,
    )
    summed = inputs.astype(jnp.float32) + to_frames(projected)
    centred = summed - jnp.mean(summed, axis=-1, keepdims=True)
    inverse = lax.rsqrt(jnp.mean(centred * centred, axis=-1, keepdims=True) + EPSILON)
    normed = centred * inverse
    conv_in = (normed * norm_gain * keep_mask).astype(jnp.bfloat16)
    padded = with_halo(conv_in, (("seq", 0),), rim_width).astype(jnp.float32)
    conv_sum = jnp.zeros((frames, utterances, width), jnp.float32)
    for offset in range(kernel_taps):
        conv_sum = conv_sum + conv_weight[offset] * padded[offset : offset + frames]
    block_out = (keep_mask * (summed + jax.nn.silu(conv_sum))).astype(jnp.bfloat16)
    grad_out = cotangent.astype(jnp.float32) * keep_mask
    sigmoid_gate = jax.nn.sigmoid(conv_sum)
    grad_conv_sum = (grad_out * sigmoid_gate * (1.0 + conv_sum * (1.0 - sigmoid_gate))).astype(
        jnp.bfloat16
    )
    grad_padded = with_halo(grad_conv_sum, (("seq", 0),), rim_width).astype(jnp.float32)
    grad_centre = grad_conv_sum.astype(jnp.float32)
    grad_conv_in = jnp.zeros((frames, utterances, width), jnp.float32)
    tap_sums = []
    for offset in range(kernel_taps):
        begin = 2 * rim_width - offset
        grad_conv_in = grad_conv_in + conv_weight[offset] * grad_padded[begin : begin + frames]
        tap_sums.append(jnp.sum(padded[offset : offset + frames] * grad_centre, axis=(0, 1)))
    grad_raw = grad_conv_in * keep_mask
    grad_conv, grad_gain = lax.psum(
        (jnp.stack(tap_sums), jnp.sum(grad_raw * normed, axis=(0, 1))), ("dp", "seq")
    )
    grad_normed = grad_raw * norm_gain
    grad_summed = (
        grad_out
        + (
            grad_normed
            - jnp.mean(grad_normed, axis=-1, keepdims=True)
            - normed * jnp.mean(grad_normed * normed, axis=-1, keepdims=True)
        )
        * inverse
    )
    grad_input = grad_summed.astype(jnp.bfloat16)
    flat_grad = grad_input.reshape(row_count, width)
    grad_flat = lax.dot_general(
        flat_grad,
        lax.all_gather(out_weight, "dp", axis=0, tiled=True),
        (((1,), (1,)), ((), ())),
        preferred_element_type=jnp.float32,
    )
    grad_attention = to_frames(grad_flat.astype(jnp.bfloat16))
    columns = flat_attn
    partial_rows = lax.psum_scatter(
        lax.dot_general(
            columns, flat_grad, (((0,), (0,)), ((), ())), preferred_element_type=jnp.float32
        ).astype(jnp.bfloat16),
        "dp",
        scatter_dimension=0,
        tiled=True,
    ).astype(jnp.float32)
    grad_weight = lax.psum(partial_rows, "seq")
    head_grad = lax.all_to_all(
        query_send(grad_attention), "seq", split_axis=0, concat_axis=0, tiled=True
    )
    grad_items = to_items(head_grad)
    grad_q, grad_k, grad_v = lax.map(
        run_backward, (query_items, key_items, value_items, item_lengths, log_totals, grad_items)
    )
    back_query = lax.all_to_all(rows_send(grad_q), "seq", split_axis=0, concat_axis=0, tiled=True)
    back_key, back_value = (
        lax.all_to_all(
            rows_send(grad_k).astype(jnp.bfloat16), "seq", split_axis=0, concat_axis=0, tiled=True
        ).astype(jnp.float32),
        lax.all_to_all(
            rows_send(grad_v).astype(jnp.bfloat16), "seq", split_axis=0, concat_axis=0, tiled=True
        ).astype(jnp.float32),
    )
    return (
        block_out,
        grad_input,
        query_back(back_query),
        whole_back(back_key).astype(jnp.bfloat16),
        whole_back(back_value).astype(jnp.bfloat16),
        grad_weight,
        grad_gain,
        grad_conv,
    )


def solution(mesh):
    in_specs = (
        P("seq", "dp", None),
        P("seq", "dp", None),
        P("seq", "dp", None),
        P("seq", "dp", None),
        P("dp"),
        P("dp", None),
        P(),
        P(),
        P("seq", "dp", None),
    )
    out_specs = (
        P("seq", "dp", None),
        P("seq", "dp", None),
        P("seq", "dp", None),
        P("seq", "dp", None),
        P("seq", "dp", None),
        P("dp", None),
        P(),
        P(),
    )
    return jax.shard_map(
        per_device, mesh=mesh, in_specs=in_specs, out_specs=out_specs, check_vma=False
    )
```

profile of v0, /device:TPU:8, one launch (start us, length us, event | category | flops | bytes accessed | tf_op | source)
XLA Modules:
  0.0 856.8 jit_solution(11271699088281422217)
XLA Ops:
  9.7 13.2 %all-to-all-start = ((bf16[64,32,1,96]{3,1,2,0:T(8,128)(2,1)}), bf16[64,32,1,96]{3,1,2,0:T(8,128)(2,1)}, u32[]{:S(2)}, u32[]{:S(2)}) async-start(bf16[64,32,1,96]{3,1,2,0:T(8,128)(2,1)} %bitcast.1), calls=%async_computation | async-start | bytes 1048576 | tf_op jit(solution)/shard_map/all_to_all | solution.py:159
  24.6 17.0 %all-to-all-done = bf16[64,32,1,96]{3,1,2,0:T(8,128)(2,1)} async-done(((bf16[64,32,1,96]{3,1,2,0:T(8,128)(2,1)}), bf16[64,32,1,96]{3,1,2,0:T(8,128)(2,1)}, u32[]{:S(2)}, u32[]{:S(2)}) %all-to-all-start) | async-done | bytes 393248 | tf_op jit(solution)/shard_map/all_to_all | solution.py:159
  42.9 5.1 all-to-all-start.1
  48.7 28.1 %all-to-all-done.1 = bf16[64,64,1,96]{3,1,2,0:T(8,128)(2,1)S(1)} async-done(((bf16[64,64,1,96]{3,1,2,0:T(8,128)(2,1)}), bf16[64,64,1,96]{3,1,2,0:T(8,128)(2,1)S(1)}, u32[]{:S(2)}, u32[]{:S(2)}) %all-to-all-start.1) | async-done | bytes 786464 | tf_op jit(solution)/shard_map/all_to_all | solution.py:163
  78.1 5.3 all-to-all-start.2
  84.9 26.5 %all-to-all-done.2 = bf16[64,64,1,96]{3,1,2,0:T(8,128)(2,1)S(1)} async-done(((bf16[64,64,1,96]{3,1,2,0:T(8,128)(2,1)}), bf16[64,64,1,96]{3,1,2,0:T(8,128)(2,1)S(1)}, u32[]{:S(2)}, u32[]{:S(2)}) %all-to-all-start.2) | async-done | bytes 786464 | tf_op jit(solution)/shard_map/all_to_all | solution.py:164
  111.5 37.2 %while.48 = (s32[]{:T(128)}, bf16[4,512,96]{1,2,0:T(8,128)(2,1)S(1)}, f32[4,512]{1,0:T(4,128)}, bf16[4,512,96]{2,1,0:T(8,128)(2,1)}, bf16[4096,96]{1,0:T(8,128)(...) while((s32[]{:T(128)}, bf16[4,512,96]{1,2,0:T(8,128)(2,1)S(1)}, ...), condition=%wide.region_4.5_spmd.clone, body=%wide.region_1.4_spmd.clone.sunk | while | flops 830524928 | bytes 27267188 | solution.py:52
  112.2 2.4 fusion.134
  114.5 2.2 fusion.135
  116.7 2.8 fusion.136
  121.5 2.4 fusion.134
  123.8 2.2 fusion.135
  126.0 2.8 fusion.136
  130.7 2.4 fusion.134
  133.1 2.1 fusion.135
  135.3 2.8 fusion.136
  140.0 2.4 fusion.134
  142.4 2.2 fusion.135
  144.6 2.8 fusion.136
  149.8 5.9 all-to-all-start.3
  156.7 15.6 %all-to-all-done.3 = bf16[64,32,1,96]{3,1,2,0:T(8,128)(2,1)S(1)} async-done(((bf16[64,32,1,96]{3,1,2,0:T(8,128)(2,1)}), bf16[64,32,1,96]{3,1,2,0:T(8,128)(2,1)S(1)}, u32[]{:S(2)}, u32[]{:S(2)}) %all-to-all-start.3) | async-done | bytes 393248 | tf_op jit(solution)/shard_map/all_to_all | solution.py:173
  173.6 3.4 fusion.104
  177.6 2.8 collective-permute-start
  180.4 7.3 collective-permute-start.1
  190.1 7.5 fusion.67
  199.6 8.5 collective-permute-start.3
  210.5 5.2 multiply_reduce_fusion.1
  219.5 4.7 convolution_convert_fusion.2
  224.2 2.2 reshape_reshape.6
  228.5 9.3 %all-to-all-start.4 = ((bf16[64,32,1,96]{3,1,2,0:T(8,128)(2,1)}), bf16[64,32,1,96]{3,1,2,0:T(8,128)(2,1)}, u32[]{:S(2)}, u32[]{:S(2)}) async-start(bf16[64,32,1,96]{3,1,2,0:T(8,128)(2,1)} %bitcast.154), calls=%async_computation.4 | async-start | bytes 1048576 | tf_op jit(solution)/shard_map/all_to_all | solution.py:238
  239.3 4.5 convolution_convert_fusion.1
  243.9 8.4 all-to-all-done.4
  253.0 117.9 %while.49 = (s32[]{:T(128)}, f32[4096,96]{0,1:T(8,128)}, f32[4096,96]{0,1:T(8,128)}, bf16[4,512,96]{1,2,0:T(8,128)(2,1)}, bf16[4,512,96]{2,1,0:T(8,128)(2,1)}, /...) while((s32[]{:T(128)}, f32[4096,96]{0,1:T(8,128)}, ...), condition=%wide.region_11.12_spmd.clone, body=%wide.region_9.11_spmd.clone.sunk | while | flops 2035863040 | bytes 106023112 | solution.py:97
  254.4 2.6 fusion.146
  257.0 6.1 multiply_reduce_fusion.6
  263.9 8.0 multiply_convert_fusion.6
  272.0 5.8 convolution_add_fusion.5
  279.8 2.9 convolution_add_fusion.4
  284.1 2.6 fusion.146
  286.7 6.0 multiply_reduce_fusion.6
  292.7 8.1 multiply_convert_fusion.6
  300.8 6.0 convolution_add_fusion.5
  308.8 3.5 convolution_add_fusion.4
  313.7 2.6 fusion.146
  316.3 5.8 multiply_reduce_fusion.6
  322.1 8.0 multiply_convert_fusion.6
  330.2 5.9 convolution_add_fusion.5
  338.1 3.5 convolution_add_fusion.4
  343.0 2.6 fusion.146
  345.6 5.8 multiply_reduce_fusion.6
  351.4 8.0 multiply_convert_fusion.6
  359.5 5.9 convolution_add_fusion.5
  367.4 3.5 convolution_add_fusion.4
  372.9 5.4 all-to-all-start.5
  378.3 2.4 copy.94
  380.8 12.1 %all-to-all-done.5 = bf16[64,32,1,96]{3,1,2,0:T(8,128)(2,1)S(1)} async-done(((bf16[64,32,1,96]{3,1,2,0:T(8,128)(2,1)}), bf16[64,32,1,96]{3,1,2,0:T(8,128)(2,1)S(1)}, u32[]{:S(2)}, u32[]{:S(2)}) %all-to-all-start.5) | async-done | bytes 393248 | tf_op jit(solution)/shard_map/all_to_all | solution.py:245
  392.9 5.0 all-to-all-start.6
  397.8 2.4 copy.97
  400.2 17.6 %all-to-all-done.6 = bf16[64,64,1,96]{3,1,2,0:T(8,128)(2,1)S(1)} async-done(((bf16[64,64,1,96]{3,1,2,0:T(8,128)(2,1)}), bf16[64,64,1,96]{3,1,2,0:T(8,128)(2,1)S(1)}, u32[]{:S(2)}, u32[]{:S(2)}) %all-to-all-start.6) | async-done | bytes 786464 | tf_op jit(solution)/shard_map/all_to_all | solution.py:247
  417.8 5.6 all-to-all-start.7
  425.6 2.8 stack.127
  428.4 2.1 copy.101
  430.6 75.7 %psum.22 = f32[1536]{0:T(1024)} all-reduce(f32[1536]{0:T(1024)S(1)} %get-tuple-element.249), channel_id=1, replica_groups=mesh['dp'=4,'seq'=64] {'dp','seq'}, use_global_device_ids=true, to_apply=%region_17.18 | all-reduce | flops 1536 | bytes 12288 | tf_op jit(solution)/shard_map/psum | solution.py:206
  514.8 333.6 %all-reduce.4 = f32[384,1536]{1,0:T(8,128)} all-reduce(bf16[384,1536]{1,0:T(8,128)(2,1)} %reduce-scatter.2.cloned.1.call-done), channel_id=1, replica_groups=mesh['dp'=4,'seq'=64] {'seq'}, use_global_device_ids=true, to_apply=%region_15.16 | all-reduce | flops 589824 | bytes 3538944 | tf_op jit(solution)/shard_map/psum | solution.py:237
  (200 shorter events, 63.4 us)
Async XLA Ops:
  7.2 40.8 %copy-start.8 = (bf16[64,2,1536]{2,1,0:T(2,128)(2,1)S(1)}, bf16[64,2,1536]{2,1,0:T(2,128)(2,1)}, u32[]{:S(2)}) copy-start(bf16[64,2,1536]{2,1,0:T(2,128)(2,1)} %param.16) | copy-start | bytes 1179652
  9.7 31.9 %all-to-all-start = ((bf16[64,32,1,96]{3,1,2,0:T(8,128)(2,1)}), bf16[64,32,1,96]{3,1,2,0:T(8,128)(2,1)}, u32[]{:S(2)}, u32[]{:S(2)}) async-start(bf16[64,32,1,96]{3,1,2,0:T(8,128)(2,1)} %bitcast.1), calls=%async_computation | async-start | bytes 1048576 | tf_op jit(solution)/shard_map/all_to_all | solution.py:159
  42.9 41.4 %copy-start.38 = (s32[2]{0:T(128)S(1)}, s32[2]{0:T(128)}, u32[]{:S(2)}) copy-start(s32[2]{0:T(128)} %param.17) | copy-start | bytes 28
  42.9 34.0 %all-to-all-start.1 = ((bf16[64,64,1,96]{3,1,2,0:T(8,128)(2,1)}), bf16[64,64,1,96]{3,1,2,0:T(8,128)(2,1)S(1)}, u32[]{:S(2)}, u32[]{:S(2)}) async-start(bf16[64,64,1,96]{3,1,2,0:T(8,128)(2,1)} %bitcast.5), calls=%async_computation.1 | async-start | bytes 2097152 | tf_op jit(solution)/shard_map/all_to_all | solution.py:163
  78.1 33.3 %all-to-all-start.2 = ((bf16[64,64,1,96]{3,1,2,0:T(8,128)(2,1)}), bf16[64,64,1,96]{3,1,2,0:T(8,128)(2,1)S(1)}, u32[]{:S(2)}, u32[]{:S(2)}) async-start(bf16[64,64,1,96]{3,1,2,0:T(8,128)(2,1)} %bitcast.9), calls=%async_computation.2 | async-start | bytes 2097152 | tf_op jit(solution)/shard_map/all_to_all | solution.py:164
  83.5 90.0 %all-gather.2.cloned.1.call-start = ((), (), s32[]{:S(2)}) async-start(), calls=%async_computation.9 | async-start | bytes 5898240 | tf_op jit(solution)/shard_map/all_gather | solution.py:179
  111.5 44.3 %copy-start.9 = (f32[31,1536]{1,0:T(8,128)S(1)}, f32[31,1536]{1,0:T(8,128)}, u32[]{:S(2)}) copy-start(f32[31,1536]{1,0:T(8,128)} %param.20) | copy-start | bytes 571396
  148.7 28.3 %copy-start.1 = (bf16[4096,96]{1,0:T(8,128)(2,1)}, bf16[4096,96]{1,0:T(8,128)(2,1)S(1)}, u32[]{:S(2)}) copy-start(bf16[4096,96]{1,0:T(8,128)(2,1)S(1)} %get-tuple-element.554) | copy-start | bytes 2359300
  149.8 22.5 %all-to-all-start.3 = ((bf16[64,32,1,96]{3,1,2,0:T(8,128)(2,1)}), bf16[64,32,1,96]{3,1,2,0:T(8,128)(2,1)S(1)}, u32[]{:S(2)}, u32[]{:S(2)}) async-start(bf16[64,32,1,96]{3,1,2,0:T(8,128)(2,1)} %bitcast.14), calls=%async_computation.3 | async-start | bytes 1048576 | tf_op jit(solution)/shard_map/all_to_all | solution.py:173
  155.7 21.5 %copy-start.10 = (f32[1536]{0:T(1024)S(1)}, f32[1536]{0:T(1024)}, u32[]{:S(2)}) copy-start(f32[1536]{0:T(1024)} %param.19) | copy-start | bytes 18436
  156.7 20.8 %copy-start.36 = (f32[64,2]{0,1:T(2,128)}, f32[64,2]{0,1:T(2,128)S(1)}, u32[]{:S(2)}) copy-start(f32[64,2]{0,1:T(2,128)S(1)} %compare_convert_fusion) | copy-start | bytes 1540
  172.7 4.9 copy-start.4
  173.5 16.6 %copy-start.7 = (bf16[64,2,1536]{2,1,0:T(2,128)(2,1)S(1)}, bf16[64,2,1536]{2,1,0:T(2,128)(2,1)}, u32[]{:S(2)}) copy-start(bf16[64,2,1536]{2,1,0:T(2,128)(2,1)} %param.21) | copy-start | bytes 1179652
  173.5 16.6 %copy-start.11 = (f32[1536]{0:T(1024)S(1)}, f32[1536]{0:T(1024)}, u32[]{:S(2)}) copy-start(f32[1536]{0:T(1024)} %get-tuple-element.295) | copy-start | bytes 18436
  173.5 16.6 %copy-start.12 = (f32[1536]{0:T(1024)S(1)}, f32[1536]{0:T(1024)}, u32[]{:S(2)}) copy-start(f32[1536]{0:T(1024)} %get-tuple-element.296) | copy-start | bytes 18436
  173.5 16.6 %copy-start.13 = (f32[1536]{0:T(1024)S(1)}, f32[1536]{0:T(1024)}, u32[]{:S(2)}) copy-start(f32[1536]{0:T(1024)} %get-tuple-element.297) | copy-start | bytes 18436
  173.5 16.6 %copy-start.14 = (f32[1536]{0:T(1024)S(1)}, f32[1536]{0:T(1024)}, u32[]{:S(2)}) copy-start(f32[1536]{0:T(1024)} %get-tuple-element.298) | copy-start | bytes 18436
  173.5 16.6 %copy-start.15 = (f32[1536]{0:T(1024)S(1)}, f32[1536]{0:T(1024)}, u32[]{:S(2)}) copy-start(f32[1536]{0:T(1024)} %get-tuple-element.299) | copy-start | bytes 18436
  173.5 16.6 %copy-start.16 = (f32[1536]{0:T(1024)S(1)}, f32[1536]{0:T(1024)}, u32[]{:S(2)}) copy-start(f32[1536]{0:T(1024)} %get-tuple-element.300) | copy-start | bytes 18436
  173.6 16.6 %copy-start.17 = (f32[1536]{0:T(1024)S(1)}, f32[1536]{0:T(1024)}, u32[]{:S(2)}) copy-start(f32[1536]{0:T(1024)} %get-tuple-element.301) | copy-start | bytes 18436
  177.6 10.7 %collective-permute-start = (bf16[15,2,1536]{2,0,1:T(8,128)(2,1)S(1)}, bf16[15,2,1536]{2,0,1:T(8,128)(2,1)S(1)}, u32[]{:S(2)}, u32[]{:S(2)}) collective-permute-start(bf16[15,2,1536]{2,0,1:T(8,128)(2,1)S(1)} %get-tuple-element.359), channel_id=1, source_target_pairs={{0,1},{1,2},{2,3},{3,4},{4,5},{5,6},{6,7},{7,8},{8,9},{9,10},{10,1... | collective-permute-start | bytes 276488 | tf_op jit(solution)/shard_map/ppermute | solution.py:21
  180.4 9.5 %collective-permute-start.1 = (bf16[15,2,1536]{2,0,1:T(8,128)(2,1)S(1)}, bf16[15,2,1536]{2,0,1:T(8,128)(2,1)S(1)}, u32[]{:S(2)}, u32[]{:S(2)}) collective-permute-start(bf16[15,2,1536]{2,0,1:T(8,128)(2,1)S(1)} %get-tuple-element.360), channel_id=1, source_target_pairs={{1,0},{2,1},{3,2},{4,3},{5,4},{6,5},{7,6},{8,7},{9,8},{10,9},{11,1... | collective-permute-start | bytes 276488 | tf_op jit(solution)/shard_map/ppermute | solution.py:22
  190.1 20.4 %copy-start.37 = (f32[64,2]{0,1:T(2,128)S(1)}, f32[64,2]{0,1:T(2,128)}, u32[]{:S(2)}) copy-start(f32[64,2]{0,1:T(2,128)} %copy-done.36) | copy-start | bytes 1540
  197.7 18.1 %copy-start.2 = (bf16[64,2,1536]{2,0,1:T(8,128)(2,1)}, bf16[64,2,1536]{2,0,1:T(8,128)(2,1)S(1)}, u32[]{:S(2)}) copy-start(bf16[64,2,1536]{2,0,1:T(8,128)(2,1)S(1)} %get-tuple-element.348) | copy-start | bytes 1179652
  197.7 11.1 %collective-permute-start.2 = (bf16[15,2,1536]{2,0,1:T(8,128)(2,1)S(1)}, bf16[15,2,1536]{2,0,1:T(8,128)(2,1)S(1)}, u32[]{:S(2)}, u32[]{:S(2)}) collective-permute-start(bf16[15,2,1536]{2,0,1:T(8,128)(2,1)S(1)} %get-tuple-element.357), channel_id=1, source_target_pairs={{0,1},{1,2},{2,3},{3,4},{4,5},{5,6},{6,7},{7,8},{8,9},{9,10},{10,1... | collective-permute-start | bytes 276488 | tf_op jit(solution)/shard_map/ppermute | solution.py:21
  199.6 10.7 %collective-permute-start.3 = (bf16[15,2,1536]{2,0,1:T(8,128)(2,1)S(1)}, bf16[15,2,1536]{2,0,1:T(8,128)(2,1)S(1)}, u32[]{:S(2)}, u32[]{:S(2)}) collective-permute-start(bf16[15,2,1536]{2,0,1:T(8,128)(2,1)S(1)} %get-tuple-element.358), channel_id=1, source_target_pairs={{1,0},{2,1},{3,2},{4,3},{5,4},{6,5},{7,6},{8,7},{9,8},{10,9},{11,1... | collective-permute-start | bytes 276488 | tf_op jit(solution)/shard_map/ppermute | solution.py:22
  218.3 19.7 %copy-start.5 = (bf16[2,32,32,1,96]{4,2,1,0,3:T(8,128)(2,1)S(1)}, bf16[2,32,32,1,96]{4,2,1,0,3:T(8,128)(2,1)}, u32[]{:S(2)}) copy-start(bf16[2,32,32,1,96]{4,2,1,0,3:T(8,128)(2,1)} %copy-done.4) | copy-start | bytes 1179652
  228.5 23.8 %all-to-all-start.4 = ((bf16[64,32,1,96]{3,1,2,0:T(8,128)(2,1)}), bf16[64,32,1,96]{3,1,2,0:T(8,128)(2,1)}, u32[]{:S(2)}, u32[]{:S(2)}) async-start(bf16[64,32,1,96]{3,1,2,0:T(8,128)(2,1)} %bitcast.154), calls=%async_computation.4 | async-start | bytes 1048576 | tf_op jit(solution)/shard_map/all_to_all | solution.py:238
  237.8 277.0 %reduce-scatter.2.cloned.1.call-start = ((), (), s32[]{:S(2)}) async-start(), calls=%async_computation.10 | async-start | bytes 5898240 | tf_op jit(solution)/shard_map/reduce_scatter | solution.py:229
  257.0 7.0 copy-start
  286.7 6.0 copy-start
  316.3 5.9 copy-start
  345.5 5.9 copy-start
  372.9 19.9 %all-to-all-start.5 = ((bf16[64,32,1,96]{3,1,2,0:T(8,128)(2,1)}), bf16[64,32,1,96]{3,1,2,0:T(8,128)(2,1)S(1)}, u32[]{:S(2)}, u32[]{:S(2)}) async-start(bf16[64,32,1,96]{3,1,2,0:T(8,128)(2,1)} %bitcast.23), calls=%async_computation.5 | async-start | bytes 1048576 | tf_op jit(solution)/shard_map/all_to_all | solution.py:245
  378.3 45.4 %copy-start.3 = (bf16[64,2,1536]{2,0,1:T(8,128)(2,1)S(1)}, bf16[64,2,1536]{2,0,1:T(8,128)(2,1)}, u32[]{:S(2)}) copy-start(bf16[64,2,1536]{2,0,1:T(8,128)(2,1)} %copy-done.2) | copy-start | bytes 1179652
  392.9 32.1 %copy-start.6 = (bf16[64,32,1,96]{3,1,2,0:T(8,128)(2,1)}, bf16[64,32,1,96]{3,1,2,0:T(8,128)(2,1)S(1)}, u32[]{:S(2)}) copy-start(bf16[64,32,1,96]{3,1,2,0:T(8,128)(2,1)S(1)} %all-to-all-done.5) | copy-start | bytes 1179652
  392.9 25.0 %all-to-all-start.6 = ((bf16[64,64,1,96]{3,1,2,0:T(8,128)(2,1)}), bf16[64,64,1,96]{3,1,2,0:T(8,128)(2,1)S(1)}, u32[]{:S(2)}, u32[]{:S(2)}) async-start(bf16[64,64,1,96]{3,1,2,0:T(8,128)(2,1)} %bitcast.149), calls=%async_computation.6 | async-start | bytes 2097152 | tf_op jit(solution)/shard_map/all_to_all | solution.py:247
  417.8 93.5 %all-to-all-start.7 = ((bf16[64,64,1,96]{3,1,2,0:T(8,128)(2,1)}), bf16[64,64,1,96]{3,1,2,0:T(8,128)(2,1)}, u32[]{:S(2)}, u32[]{:S(2)}) async-start(bf16[64,64,1,96]{3,1,2,0:T(8,128)(2,1)} %bitcast.148), calls=%async_computation.7 | async-start | bytes 2097152 | tf_op jit(solution)/shard_map/all_to_all | solution.py:250
  423.5 1.5 copy-start.35
  423.5 1.5 copy-start.34
  423.5 1.6 copy-start.33
  423.5 1.6 copy-start.32
  423.5 1.6 copy-start.31
  423.5 1.6 copy-start.30
  423.6 1.6 copy-start.29
  423.6 1.6 copy-start.28
  423.6 1.6 copy-start.27
  423.6 1.7 copy-start.26
  423.6 1.7 copy-start.25
  423.6 1.7 copy-start.24
  423.6 1.7 copy-start.23
  423.6 1.7 copy-start.22
  423.6 1.7 copy-start.21
  423.6 1.7 copy-start.20
  423.7 1.8 copy-start.19
  423.7 1.8 copy-start.18
  423.7 424.7 %all-reduce.3.cloned.1.call-start = ((), (), s32[]{:S(2)}) async-start(), calls=%async_computation.11 | async-start | bytes 393216 | tf_op jit(solution)/shard_map/psum | solution.py:206
Sparse Core Ops, SparseCore 0:
  86.1 47.8 all-gather.1
  244.0 59.9 reduce-scatter.1
  431.5 247.2 all-reduce.2
where the time goes:
time: 867 us; the launch traced here: 857 us
  blocking collectives  409 us (47%)
  waiting for transfers between devices  130 us (15%)
  matrix products  113 us (13%)
  starting transfers between devices  75.6 us (9%)
  other arithmetic  64.8 us (7%)
  local copies, waits for them, and re-layouts  48.9 us (6%)
  between operations  15.1 us (2%)
    psum x1, blocking collectives, per_device(): grad_weight = lax.psum(partial_rows, 'seq')  334 us
    psum x1, blocking collectives, per_device(): lax.psum((jnp.stack(tap_sums), jnp.sum(grad_raw * normed, axis=(0, 1))),...  75.7 us
    convert_element_type x4, other arithmetic, block_step(): (probs * (grad_probs - centre) * score_scale).astype(jnp.bfloat16)  32.3 us
    all_to_all x1, waiting for transfers between devices, per_device(): lax.all_to_all(whole_send(key_proj), 'seq', split_axis=0, concat_axis=0,...  28.1 us
    all_to_all x1, waiting for transfers between devices, per_device(): lax.all_to_all(whole_send(value_proj), 'seq', split_axis=0, concat_axis=0...  26.5 us
    dot_general x4, matrix products, block_step(): jnp.einsum('qd,kd->qk', query_block, key_item, preferred_element_type=jnp...  23.7 us
    dot_general x4, matrix products, block_step(): jnp.einsum('qk,qd->kd', probs_low, grad_block, preferred_element_type=jnp...  23.5 us
    all_to_all x1, waiting for transfers between devices, per_device(): lax.all_to_all(rows_send(grad_k).astype(jnp.bfloat16), 'seq', split_axis=...  17.6 us
  transfers between devices with their start and end apart: 15, of which 11 were waited for; matrix products, arithmetic and copies ran while one was open for 22% of the time, Pallas kernels for 0%

commit v1 on v0

--- a/solution.py
+++ b/solution.py
@@ -3,6 +3,7 @@
 import jax
 import jax.numpy as jnp
 from jax import lax
+from jax.sharding import Mesh
 from jax.sharding import PartitionSpec as P
 
 H = 16
@@ -24,6 +25,58 @@
     return shard
 
 
+SEQ = ("yl", "x", "z")
+DP = ("yh", "c")
+SWAP = [(0, 1), (1, 0)]
+
+
+def split_halves(total):
+    high = total.astype(jnp.bfloat16)
+    return high, (total - high.astype(jnp.float32)).astype(jnp.bfloat16)
+
+
+def sum_parameters(flat_attn, flat_grad, small):
+    core = lax.axis_index("c")
+    width = flat_attn.shape[1]
+    block = width // 4
+    by_core = flat_attn.reshape(-1, 2, 2, block)
+    mine = lax.dynamic_index_in_dim(by_core, core, axis=2, keepdims=False)
+    theirs = lax.dynamic_index_in_dim(by_core, 1 - core, axis=2, keepdims=False)
+    other_attn = lax.ppermute(theirs.reshape(-1, 2 * block), "c", SWAP)
+    other_grad = lax.ppermute(flat_grad, "c", SWAP)
+    small = small + lax.ppermute(small, "c", SWAP)
+    rows = jnp.concatenate([mine.reshape(-1, 2 * block), other_attn])
+    grads = jnp.concatenate([flat_grad, other_grad])
+    partial = lax.dot_general(
+        rows, grads, (((0,), (0,)), ((), ())), preferred_element_type=jnp.float32
+    ).astype(jnp.bfloat16)
+    count = small.shape[0] // 8
+    high, low = split_halves(small)
+    small_blocks = jnp.concatenate(
+        [high.reshape(8, count, width), low.reshape(8, count, width)], axis=1
+    )
+    sent = jnp.concatenate(
+        [partial.reshape(16, block // 8, width), jnp.tile(small_blocks, (2, 1, 1))], axis=1
+    )
+    got = lax.all_to_all(sent, ("yh", "yl", "x"), 0, 0, tiled=True)
+    total = jnp.sum(got.astype(jnp.float32), axis=0)
+    big = total[: block // 8].astype(jnp.bfloat16).reshape(8, block // 64, width)
+    high, low = split_halves(total[block // 8 : block // 8 + count] + total[block // 8 + count :])
+    tail = jnp.broadcast_to(jnp.concatenate([high, low])[None], (8, 2 * count, width))
+    got = lax.all_to_all(jnp.concatenate([big, tail], axis=1), "z", 0, 0, tiled=True)
+    total = jnp.sum(got.astype(jnp.float32), axis=0)
+    final = total[: block // 64].astype(jnp.bfloat16)
+    high, low = split_halves(total[block // 64 : block // 64 + count] + total[block // 64 + count :])
+    got = lax.all_to_all(jnp.broadcast_to(final[None], (8,) + final.shape), "z", 0, 0, tiled=True)
+    piece = jnp.concatenate([got.reshape(block // 8, width), high, low])
+    got = lax.all_to_all(
+        jnp.broadcast_to(piece[None], (8,) + piece.shape), ("yl", "x"), 0, 0, tiled=True
+    ).astype(jnp.float32)
+    grad_weight = got[:, : block // 8].reshape(block, width)
+    small = (got[:, block // 8 : block // 8 + count] + got[:, block // 8 + count :]).reshape(-1, width)
+    return grad_weight, small[:-1], small[-1]
+
+
 def block_size():
     return 512
 
@@ -112,7 +165,7 @@
     inputs, query_proj, key_proj, value_proj, lengths, out_weight, norm_gain, conv_weight, cotangent
 ):
     frames, utterances, width = inputs.shape
-    groups = lax.axis_size("seq")
+    groups = lax.axis_size(SEQ)
     head_width = width // H
     pair_count = utterances * H
     item_count = max(1, pair_count // groups)
@@ -122,9 +175,9 @@
     row_count = frames * utterances
     kernel_taps = conv_weight.shape[0]
     rim_width = (kernel_taps - 1) // 2
-    position = lax.axis_index("seq") * frames + jnp.arange(frames)
+    position = lax.axis_index(SEQ) * frames + jnp.arange(frames)
     keep_mask = (position[:, None] < lengths[None, :]).astype(jnp.float32)[:, :, None]
-    item_ids = lax.axis_index("seq") // query_split * item_count + jnp.arange(item_count)
+    item_ids = lax.axis_index(SEQ) // query_split * item_count + jnp.arange(item_count)
     owner_pick = (item_ids // H)[:, None] == jnp.arange(utterances)[None, :]
     item_lengths = jnp.sum(jnp.where(owner_pick, lengths[None, :], 0), axis=1)
 
@@ -157,11 +210,11 @@
         return tensor.reshape(frames, utterances, width)
 
     head_query = lax.all_to_all(
-        query_send(query_proj), "seq", split_axis=0, concat_axis=0, tiled=True
+        query_send(query_proj), SEQ, split_axis=0, concat_axis=0, tiled=True
     )
     head_key, head_value = (
-        lax.all_to_all(whole_send(key_proj), "seq", split_axis=0, concat_axis=0, tiled=True),
-        lax.all_to_all(whole_send(value_proj), "seq", split_axis=0, concat_axis=0, tiled=True),
+        lax.all_to_all(whole_send(key_proj), SEQ, split_axis=0, concat_axis=0, tiled=True),
+        lax.all_to_all(whole_send(value_proj), SEQ, split_axis=0, concat_axis=0, tiled=True),
     )
     query_items = to_items(head_query)
     key_items = to_items(head_key)
@@ -170,13 +223,13 @@
         run_forward, (query_items, key_items, value_items, item_lengths)
     )
     attention = query_back(
-        lax.all_to_all(rows_send(mixed_items), "seq", split_axis=0, concat_axis=0, tiled=True)
+        lax.all_to_all(rows_send(mixed_items), SEQ, split_axis=0, concat_axis=0, tiled=True)
     )
     flat_attn = attention.reshape(row_count, width)
     columns = flat_attn
     projected = jnp.dot(
         columns,
-        lax.all_gather(out_weight, "dp", axis=0, tiled=True),
+        lax.all_gather(out_weight, DP, axis=0, tiled=True),
         preferred_element_type=jnp.float32,
     )
     summed = inputs.astype(jnp.float32) + to_frames(projected)
@@ -184,7 +237,7 @@
     inverse = lax.rsqrt(jnp.mean(centred * centred, axis=-1, keepdims=True) + EPSILON)
     normed = centred * inverse
     conv_in = (normed * norm_gain * keep_mask).astype(jnp.bfloat16)
-    padded = with_halo(conv_in, (("seq", 0),), rim_width).astype(jnp.float32)
+    padded = with_halo(conv_in, ((SEQ, 0),), rim_width).astype(jnp.float32)
     conv_sum = jnp.zeros((frames, utterances, width), jnp.float32)
     for offset in range(kernel_taps):
         conv_sum = conv_sum + conv_weight[offset] * padded[offset : offset + frames]
@@ -194,7 +247,7 @@
     grad_conv_sum = (grad_out * sigmoid_gate * (1.0 + conv_sum * (1.0 - sigmoid_gate))).astype(
         jnp.bfloat16
     )
-    grad_padded = with_halo(grad_conv_sum, (("seq", 0),), rim_width).astype(jnp.float32)
+    grad_padded = with_halo(grad_conv_sum, ((SEQ, 0),), rim_width).astype(jnp.float32)
     grad_centre = grad_conv_sum.astype(jnp.float32)
     grad_conv_in = jnp.zeros((frames, utterances, width), jnp.float32)
     tap_sums = []
@@ -203,9 +256,7 @@
         grad_conv_in = grad_conv_in + conv_weight[offset] * grad_padded[begin : begin + frames]
         tap_sums.append(jnp.sum(padded[offset : offset + frames] * grad_centre, axis=(0, 1)))
     grad_raw = grad_conv_in * keep_mask
-    grad_conv, grad_gain = lax.psum(
-        (jnp.stack(tap_sums), jnp.sum(grad_raw * normed, axis=(0, 1))), ("dp", "seq")
-    )
+    small = jnp.concatenate([jnp.stack(tap_sums), jnp.sum(grad_raw * normed, axis=(0, 1))[None]])
     grad_normed = grad_raw * norm_gain
     grad_summed = (
         grad_out
@@ -220,35 +271,27 @@
     flat_grad = grad_input.reshape(row_count, width)
     grad_flat = lax.dot_general(
         flat_grad,
-        lax.all_gather(out_weight, "dp", axis=0, tiled=True),
+        lax.all_gather(out_weight, DP, axis=0, tiled=True),
         (((1,), (1,)), ((), ())),
         preferred_element_type=jnp.float32,
     )
     grad_attention = to_frames(grad_flat.astype(jnp.bfloat16))
     columns = flat_attn
-    partial_rows = lax.psum_scatter(
-        lax.dot_general(
-            columns, flat_grad, (((0,), (0,)), ((), ())), preferred_element_type=jnp.float32
-        ).astype(jnp.bfloat16),
-        "dp",
-        scatter_dimension=0,
-        tiled=True,
-    ).astype(jnp.float32)
-    grad_weight = lax.psum(partial_rows, "seq")
+    grad_weight, grad_conv, grad_gain = sum_parameters(flat_attn, flat_grad, small)
     head_grad = lax.all_to_all(
-        query_send(grad_attention), "seq", split_axis=0, concat_axis=0, tiled=True
+        query_send(grad_attention), SEQ, split_axis=0, concat_axis=0, tiled=True
     )
     grad_items = to_items(head_grad)
     grad_q, grad_k, grad_v = lax.map(
         run_backward, (query_items, key_items, value_items, item_lengths, log_totals, grad_items)
     )
-    back_query = lax.all_to_all(rows_send(grad_q), "seq", split_axis=0, concat_axis=0, tiled=True)
+    back_query = lax.all_to_all(rows_send(grad_q), SEQ, split_axis=0, concat_axis=0, tiled=True)
     back_key, back_value = (
         lax.all_to_all(
-            rows_send(grad_k).astype(jnp.bfloat16), "seq", split_axis=0, concat_axis=0, tiled=True
+            rows_send(grad_k).astype(jnp.bfloat16), SEQ, split_axis=0, concat_axis=0, tiled=True
         ).astype(jnp.float32),
         lax.all_to_all(
-            rows_send(grad_v).astype(jnp.bfloat16), "seq", split_axis=0, concat_axis=0, tiled=True
+            rows_send(grad_v).astype(jnp.bfloat16), SEQ, split_axis=0, concat_axis=0, tiled=True
         ).astype(jnp.float32),
     )
     return (
@@ -264,24 +307,25 @@
 
 
 def solution(mesh):
+    mesh = Mesh(mesh.devices.reshape(2, 2, 2, 4, 8), ("yh", "c", "yl", "x", "z"))
     in_specs = (
-        P("seq", "dp", None),
-        P("seq", "dp", None),
-        P("seq", "dp", None),
-        P("seq", "dp", None),
-        P("dp"),
-        P("dp", None),
+        P(SEQ, DP, None),
+        P(SEQ, DP, None),
+        P(SEQ, DP, None),
+        P(SEQ, DP, None),
+        P(DP),
+        P(DP, None),
         P(),
         P(),
-        P("seq", "dp", None),
+        P(SEQ, DP, None),
     )
     out_specs = (
-        P("seq", "dp", None),
-        P("seq", "dp", None),
-        P("seq", "dp", None),
-        P("seq", "dp", None),
-        P("seq", "dp", None),
-        P("dp", None),
+        P(SEQ, DP, None),
+        P(SEQ, DP, None),
+        P(SEQ, DP, None),
+        P(SEQ, DP, None),
+        P(SEQ, DP, None),
+        P(DP, None),
         P(),
         P(),
     )

time: 867 us -> 550 us (0.63)
  blocking collectives: 409 us -> 0 us
  waiting for transfers between devices: 130 us -> 182 us
  local copies, waits for them, and re-layouts: 48.9 us -> 73.3 us
  starting transfers between devices: 75.6 us -> 90.7 us
    psum x2 -> x0, blocking collectives: 409 us -> none  [the longest x1 334 us: per_device(): grad_weight = lax.psum(partial_rows, 'seq')]
    all_to_all x8 -> x12, waiting for transfers between devices: 125 us -> 181 us  [the longest x1 28.1 us: per_device(): lax.all_to_all(whole_send(key_proj), SEQ, split_axis=0, concat_axis=0, ti...]
    another operation x32 -> x31, local copies, waits for them, and re-layouts: 2.96 us -> 18.5 us  [per_device(): jnp.stack(tap_sums)]
    all_to_all x8 -> x12, starting transfers between devices: 54.8 us -> 69.6 us  [the longest x1 13.2 us: per_device(): lax.all_to_all(query_send(query_proj), SEQ, split_axis=0, concat_axis=0,...]
  transfers between devices with their start and end apart: 15 -> 20, of which waited for: 11 -> 11; matrix products, arithmetic and copies ran while one was open for 22% -> 43% of each run, Pallas kernels for 0% -> 0%
where the time goes in v1:
time: 550 us; the launch traced here: 539 us
  waiting for transfers between devices  182 us (33%)
  matrix products  105 us (19%)
  starting transfers between devices  90.7 us (16%)
  local copies, waits for them, and re-layouts  73.3 us (13%)
  other arithmetic  72.4 us (13%)
  between operations  16 us (3%)
    convert_element_type x4, other arithmetic, block_step(): (probs * (grad_probs - centre) * score_scale).astype(jnp.bfloat16)  32.2 us
    all_to_all x1, waiting for transfers between devices, per_device(): lax.all_to_all(whole_send(key_proj), SEQ, split_axis=0, concat_axis=0, ti...  28.1 us
    all_to_all x1, waiting for transfers between devices, per_device(): lax.all_to_all(whole_send(value_proj), SEQ, split_axis=0, concat_axis=0,...  26.5 us
    all_to_all x1, waiting for transfers between devices, per_device(): lax.all_to_all(rows_send(grad_k).astype(jnp.bfloat16), SEQ, split_axis=0,...  25.3 us
    dot_general x4, matrix products, block_step(): jnp.einsum('qd,kd->qk', query_block, key_item, preferred_element_type=jnp...  23.4 us
    dot_general x4, matrix products, block_step(): jnp.einsum('qk,qd->kd', probs_low, grad_block, preferred_element_type=jnp...  23.1 us
    all_to_all x1, waiting for transfers between devices, per_device(): lax.all_to_all(rows_send(grad_v).astype(jnp.bfloat16), SEQ, split_axis=0,...  22.2 us
    another operation x31, local copies, waits for them, and re-layouts, per_device(): jnp.stack(tap_sums)  18.5 us
  transfers between devices with their start and end apart: 20, of which 11 were waited for; matrix products, arithmetic and copies ran while one was open for 43% of the time, Pallas kernels for 0%

profile of v1, /device:TPU:8, one launch (start us, length us, event | category | flops | bytes accessed | tf_op | source)
XLA Modules:
  0.0 539.3 jit_solution(8011634291549799700)
XLA Ops:
  9.7 13.2 %all-to-all-start = ((bf16[64,32,1,96]{3,1,2,0:T(8,128)(2,1)}), bf16[64,32,1,96]{3,1,2,0:T(8,128)(2,1)}, u32[]{:S(2)}, u32[]{:S(2)}) async-start(bf16[64,32,1,96]{3,1,2,0:T(8,128)(2,1)} %bitcast.1), calls=%async_computation | async-start | bytes 1048576 | tf_op jit(solution)/shard_map/all_to_all | solution.py:212
  24.6 17.0 %all-to-all-done = bf16[64,32,1,96]{3,1,2,0:T(8,128)(2,1)} async-done(((bf16[64,32,1,96]{3,1,2,0:T(8,128)(2,1)}), bf16[64,32,1,96]{3,1,2,0:T(8,128)(2,1)}, u32[]{:S(2)}, u32[]{:S(2)}) %all-to-all-start) | async-done | bytes 393248 | tf_op jit(solution)/shard_map/all_to_all | solution.py:212
  42.9 5.1 all-to-all-start.1
  48.7 28.1 %all-to-all-done.1 = bf16[64,64,1,96]{3,1,2,0:T(8,128)(2,1)S(1)} async-done(((bf16[64,64,1,96]{3,1,2,0:T(8,128)(2,1)}), bf16[64,64,1,96]{3,1,2,0:T(8,128)(2,1)S(1)}, u32[]{:S(2)}, u32[]{:S(2)}) %all-to-all-start.1) | async-done | bytes 786464 | tf_op jit(solution)/shard_map/all_to_all | solution.py:216
  78.1 5.3 all-to-all-start.2
  84.9 26.5 %all-to-all-done.2 = bf16[64,64,1,96]{3,1,2,0:T(8,128)(2,1)S(1)} async-done(((bf16[64,64,1,96]{3,1,2,0:T(8,128)(2,1)}), bf16[64,64,1,96]{3,1,2,0:T(8,128)(2,1)S(1)}, u32[]{:S(2)}, u32[]{:S(2)}) %all-to-all-start.2) | async-done | bytes 786464 | tf_op jit(solution)/shard_map/all_to_all | solution.py:217
  111.5 36.9 %while.48 = (s32[]{:T(128)}, bf16[4,512,96]{1,2,0:T(8,128)(2,1)S(1)}, f32[4,512]{1,0:T(4,128)}, bf16[4,512,96]{2,1,0:T(8,128)(2,1)}, bf16[4096,96]{1,0:T(8,128)(...) while((s32[]{:T(128)}, bf16[4,512,96]{1,2,0:T(8,128)(2,1)S(1)}, ...), condition=%wide.region_4.5_spmd.clone, body=%wide.region_1.4_spmd.clone.sunk | while | flops 830524928 | bytes 27267188 | solution.py:105
  112.1 2.4 fusion.143
  114.5 2.2 fusion.144
  116.6 2.8 fusion.145
  121.3 2.4 fusion.143
  125.8 2.8 fusion.145
  130.5 2.4 fusion.143
  135.0 2.8 fusion.145
  139.7 2.4 fusion.143
  144.3 2.8 fusion.145
  149.4 5.9 %all-to-all-start.3 = ((bf16[64,32,1,96]{3,1,2,0:T(8,128)(2,1)}), bf16[64,32,1,96]{3,1,2,0:T(8,128)(2,1)S(1)}, u32[]{:S(2)}, u32[]{:S(2)}) async-start(bf16[64,32,1,96]{3,1,2,0:T(8,128)(2,1)} %bitcast.14), calls=%async_computation.3 | async-start | bytes 1048576 | tf_op jit(solution)/shard_map/all_to_all | solution.py:226
  157.1 14.8 %all-to-all-done.3 = bf16[64,32,1,96]{3,1,2,0:T(8,128)(2,1)S(1)} async-done(((bf16[64,32,1,96]{3,1,2,0:T(8,128)(2,1)}), bf16[64,32,1,96]{3,1,2,0:T(8,128)(2,1)S(1)}, u32[]{:S(2)}, u32[]{:S(2)}) %all-to-all-start.3) | async-done | bytes 393248 | tf_op jit(solution)/shard_map/all_to_all | solution.py:226
  176.6 3.4 fusion.115
  182.0 2.8 collective-permute-start
  184.8 7.2 %collective-permute-start.1 = (bf16[15,2,1536]{2,0,1:T(8,128)(2,1)}, bf16[15,2,1536]{2,0,1:T(8,128)(2,1)S(1)}, u32[]{:S(2)}, u32[]{:S(2)}) collective-permute-start(bf16[15,2,1536]{2,0,1:T(8,128)(2,1)} %get-tuple-element.392), channel_id=1, source_target_pairs={{1,0},{2,1},{3,2},{4,3},{5,4},{6,5},{7,6},{8,7},{9,8},{10,9},{11,1... | collective-permute-start | bytes 276488 | tf_op jit(solution)/shard_map/ppermute | solution.py:23
  198.6 7.1 %fusion.67 = (f32[1536]{0:T(1024)S(1)}, f32[1536]{0:T(1024)S(1)}, f32[1536]{0:T(1024)S(1)}, f32[1536]{0:T(1024)S(1)}, f32[1536]{0:T(1024)S(1)}, /*index=5*/f32[1...) fusion(f32[94,2,1536]{2,0,1:T(8,128)S(1)} %maximum_convert_fusi, ...), kind=kLoop, calls=%fused_computation.111 | loop fusion | flops 21402624 | bytes 26253824 | tf_op jit(solution)/shard_map/reduce_sum | solution.py:257
  207.9 8.4 %collective-permute-start.3 = (bf16[15,2,1536]{2,0,1:T(8,128)(2,1)S(1)}, bf16[15,2,1536]{2,0,1:T(8,128)(2,1)S(1)}, u32[]{:S(2)}, u32[]{:S(2)}) collective-permute-start(bf16[15,2,1536]{2,0,1:T(8,128)(2,1)S(1)} %get-tuple-element.390), channel_id=1, source_target_pairs={{1,0},{2,1},{3,2},{4,3},{5,4},{6,5},{7,6},{8,7},{9,8},{10,9},{11,1... | collective-permute-start | bytes 276488 | tf_op jit(solution)/shard_map/ppermute | solution.py:23
  236.5 5.2 multiply_reduce_fusion.1
  244.2 2.8 concatenate.34
  247.7 4.7 convolution_convert_fusion.2
  254.9 5.1 all-to-all-start.4
  265.0 12.9 %all-to-all-done.4 = bf16[64,32,1,96]{3,1,2,0:T(8,128)(2,1)} async-done(((bf16[64,32,1,96]{3,1,2,0:T(8,128)(2,1)}), bf16[64,32,1,96]{3,1,2,0:T(8,128)(2,1)}, u32[]{:S(2)}, u32[]{:S(2)}) %all-to-all-start.4) | async-done | bytes 393248 | tf_op jit(solution)/shard_map/all_to_all | solution.py:281
  277.9 6.5 %all-to-all-start.8 = ((bf16[16,56,1536]{2,1,0:T(8,128)(2,1)}), bf16[16,56,1536]{2,1,0:T(8,128)(2,1)}, u32[]{:S(2)}, u32[]{:S(2)}) async-start(bf16[16,56,1536]{2,1,0:T(8,128)(2,1)} %pad_maximum_fusion), calls=%async_computation.8 | async-start | bytes 5505024 | tf_op jit(solution)/shard_map/all_to_all | solution.py:61
  284.5 111.7 %while.49 = (s32[]{:T(128)}, f32[4096,96]{0,1:T(8,128)}, f32[4096,96]{0,1:T(8,128)}, bf16[4,512,96]{1,2,0:T(8,128)(2,1)S(1)}, bf16[4,512,96]{2,1,0:T(8,128)(2,1)...) while((s32[]{:T(128)}, f32[4096,96]{0,1:T(8,128)}, ...), condition=%wide.region_11.12_spmd.clone, body=%wide.region_9.11_spmd.clone.sunk | while | flops 2035863040 | bytes 106023112 | solution.py:150
  285.8 2.2 fusion.155
  288.0 5.8 %multiply_reduce_fusion.6 = (f32[512]{0:T(512)S(1)}, f32[512,4096]{1,0:T(8,128)}) fusion(f32[512,4096]{1,0:T(8,128)S(1)} %fusion.155, f32[512]{0:T(512)S(1)} %bitcast.168, bf16[4096,96]{1,0:T(8,128)(2,1)S(1)} %get-tuple-element.565, bf16[4,512,96]{2,1,0:T(8,128)(2,1)} %get-tuple-element.564, s32[]{:T(128)S(6)} %copy.217, ...), kind=kOutput, calls=%fused_computation.20.clone.1 | convolution fusion | flops 413138432 | bytes 17702916 | tf_op jit(solution)/shard_map/while/body/eval_jaxpr/while/body/eval_jaxpr/qd,kd->qk/dot_general | solution.py:122
  293.9 8.0 %multiply_convert_fusion.6 = bf16[512,4096]{1,0:T(8,128)(2,1)S(1)} fusion(f32[512,4096]{1,0:T(8,128)} %get-tuple-element.507, f32[512,4096]{1,0:T(8,128)} %copy-done, f32[512]{0:T(512)S(1)} %get-tuple-element.508), kind=kLoop, calls=%fused_computation.19.clone.1 | loop fusion | flops 8388608 | bytes 20973568 | tf_op jit(solution)/shard_map/while/body/eval_jaxpr/while/body/eval_jaxpr/convert_element_type | solution.py:135
  301.9 5.4 %convolution_add_fusion.5 = f32[4096,96]{0,1:T(8,128)} fusion(f32[512,4096]{1,0:T(8,128)} %get-tuple-element.507, f32[4096,96]{0,1:T(8,128)} %get-tuple-element.550, pred[]{:T(512)S(6)} %compare.7, bf16[4,512,96]{2,1,0:T(8,128)(2,1)} %get-tuple-element.567, s32[]{:T(128)S(6)} %copy.217), kind=kOutput, calls=%fused_computation.22.clone.1 | convolution fusion | flops 405536768 | bytes 11665413 | tf_op jit(solution)/shard_map/while/body/eval_jaxpr/while/body/eval_jaxpr/qk,qd->kd/dot_general | solution.py:128
  308.7 3.0 convolution_add_fusion.4
  313.0 2.2 fusion.155
  315.2 5.8 %multiply_reduce_fusion.6 = (f32[512]{0:T(512)S(1)}, f32[512,4096]{1,0:T(8,128)}) fusion(f32[512,4096]{1,0:T(8,128)S(1)} %fusion.155, f32[512]{0:T(512)S(1)} %bitcast.168, bf16[4096,96]{1,0:T(8,128)(2,1)S(1)} %get-tuple-element.565, bf16[4,512,96]{2,1,0:T(8,128)(2,1)} %get-tuple-element.564, s32[]{:T(128)S(6)} %copy.217, ...), kind=kOutput, calls=%fused_computation.20.clone.1 | convolution fusion | flops 413138432 | bytes 17702916 | tf_op jit(solution)/shard_map/while/body/eval_jaxpr/while/body/eval_jaxpr/qd,kd->qk/dot_general | solution.py:122
  321.0 8.0 %multiply_convert_fusion.6 = bf16[512,4096]{1,0:T(8,128)(2,1)S(1)} fusion(f32[512,4096]{1,0:T(8,128)} %get-tuple-element.507, f32[512,4096]{1,0:T(8,128)} %copy-done, f32[512]{0:T(512)S(1)} %get-tuple-element.508), kind=kLoop, calls=%fused_computation.19.clone.1 | loop fusion | flops 8388608 | bytes 20973568 | tf_op jit(solution)/shard_map/while/body/eval_jaxpr/while/body/eval_jaxpr/convert_element_type | solution.py:135
  329.1 5.9 %convolution_add_fusion.5 = f32[4096,96]{0,1:T(8,128)} fusion(f32[512,4096]{1,0:T(8,128)} %get-tuple-element.507, f32[4096,96]{0,1:T(8,128)} %get-tuple-element.550, pred[]{:T(512)S(6)} %compare.7, bf16[4,512,96]{2,1,0:T(8,128)(2,1)} %get-tuple-element.567, s32[]{:T(128)S(6)} %copy.217), kind=kOutput, calls=%fused_computation.22.clone.1 | convolution fusion | flops 405536768 | bytes 11665413 | tf_op jit(solution)/shard_map/while/body/eval_jaxpr/while/body/eval_jaxpr/qk,qd->kd/dot_general | solution.py:128
  336.3 3.5 convolution_add_fusion.4
  341.1 2.2 fusion.155
  343.3 5.8 %multiply_reduce_fusion.6 = (f32[512]{0:T(512)S(1)}, f32[512,4096]{1,0:T(8,128)}) fusion(f32[512,4096]{1,0:T(8,128)S(1)} %fusion.155, f32[512]{0:T(512)S(1)} %bitcast.168, bf16[4096,96]{1,0:T(8,128)(2,1)S(1)} %get-tuple-element.565, bf16[4,512,96]{2,1,0:T(8,128)(2,1)} %get-tuple-element.564, s32[]{:T(128)S(6)} %copy.217, ...), kind=kOutput, calls=%fused_computation.20.clone.1 | convolution fusion | flops 413138432 | bytes 17702916 | tf_op jit(solution)/shard_map/while/body/eval_jaxpr/while/body/eval_jaxpr/qd,kd->qk/dot_general | solution.py:122
  349.2 8.0 %multiply_convert_fusion.6 = bf16[512,4096]{1,0:T(8,128)(2,1)S(1)} fusion(f32[512,4096]{1,0:T(8,128)} %get-tuple-element.507, f32[512,4096]{1,0:T(8,128)} %copy-done, f32[512]{0:T(512)S(1)} %get-tuple-element.508), kind=kLoop, calls=%fused_computation.19.clone.1 | loop fusion | flops 8388608 | bytes 20973568 | tf_op jit(solution)/shard_map/while/body/eval_jaxpr/while/body/eval_jaxpr/convert_element_type | solution.py:135
  357.2 5.9 %convolution_add_fusion.5 = f32[4096,96]{0,1:T(8,128)} fusion(f32[512,4096]{1,0:T(8,128)} %get-tuple-element.507, f32[4096,96]{0,1:T(8,128)} %get-tuple-element.550, pred[]{:T(512)S(6)} %compare.7, bf16[4,512,96]{2,1,0:T(8,128)(2,1)} %get-tuple-element.567, s32[]{:T(128)S(6)} %copy.217), kind=kOutput, calls=%fused_computation.22.clone.1 | convolution fusion | flops 405536768 | bytes 11665413 | tf_op jit(solution)/shard_map/while/body/eval_jaxpr/while/body/eval_jaxpr/qk,qd->kd/dot_general | solution.py:128
  364.5 3.5 convolution_add_fusion.4
  369.3 2.2 fusion.155
  371.5 5.8 %multiply_reduce_fusion.6 = (f32[512]{0:T(512)S(1)}, f32[512,4096]{1,0:T(8,128)}) fusion(f32[512,4096]{1,0:T(8,128)S(1)} %fusion.155, f32[512]{0:T(512)S(1)} %bitcast.168, bf16[4096,96]{1,0:T(8,128)(2,1)S(1)} %get-tuple-element.565, bf16[4,512,96]{2,1,0:T(8,128)(2,1)} %get-tuple-element.564, s32[]{:T(128)S(6)} %copy.217, ...), kind=kOutput, calls=%fused_computation.20.clone.1 | convolution fusion | flops 413138432 | bytes 17702916 | tf_op jit(solution)/shard_map/while/body/eval_jaxpr/while/body/eval_jaxpr/qd,kd->qk/dot_general | solution.py:122
  377.3 8.0 %multiply_convert_fusion.6 = bf16[512,4096]{1,0:T(8,128)(2,1)S(1)} fusion(f32[512,4096]{1,0:T(8,128)} %get-tuple-element.507, f32[512,4096]{1,0:T(8,128)} %copy-done, f32[512]{0:T(512)S(1)} %get-tuple-element.508), kind=kLoop, calls=%fused_computation.19.clone.1 | loop fusion | flops 8388608 | bytes 20973568 | tf_op jit(solution)/shard_map/while/body/eval_jaxpr/while/body/eval_jaxpr/convert_element_type | solution.py:135
  385.4 5.9 %convolution_add_fusion.5 = f32[4096,96]{0,1:T(8,128)} fusion(f32[512,4096]{1,0:T(8,128)} %get-tuple-element.507, f32[4096,96]{0,1:T(8,128)} %get-tuple-element.550, pred[]{:T(512)S(6)} %compare.7, bf16[4,512,96]{2,1,0:T(8,128)(2,1)} %get-tuple-element.567, s32[]{:T(128)S(6)} %copy.217), kind=kOutput, calls=%fused_computation.22.clone.1 | convolution fusion | flops 405536768 | bytes 11665413 | tf_op jit(solution)/shard_map/while/body/eval_jaxpr/while/body/eval_jaxpr/qk,qd->kd/dot_general | solution.py:128
  392.7 3.5 convolution_add_fusion.4
  397.2 6.7 %all-to-all-start.5 = ((bf16[64,32,1,96]{3,1,2,0:T(8,128)(2,1)}), bf16[64,32,1,96]{3,1,2,0:T(8,128)(2,1)S(1)}, u32[]{:S(2)}, u32[]{:S(2)}) async-start(bf16[64,32,1,96]{3,1,2,0:T(8,128)(2,1)} %bitcast.23), calls=%async_computation.5 | async-start | bytes 1048576 | tf_op jit(solution)/shard_map/all_to_all | solution.py:288
  403.9 2.2 convert_reduce_fusion
  407.2 14.3 %all-to-all-done.5 = bf16[64,32,1,96]{3,1,2,0:T(8,128)(2,1)S(1)} async-done(((bf16[64,32,1,96]{3,1,2,0:T(8,128)(2,1)}), bf16[64,32,1,96]{3,1,2,0:T(8,128)(2,1)S(1)}, u32[]{:S(2)}, u32[]{:S(2)}) %all-to-all-start.5) | async-done | bytes 393248 | tf_op jit(solution)/shard_map/all_to_all | solution.py:288
  421.5 3.5 all-to-all-start.9
  424.9 2.4 copy.180
  427.3 9.4 %all-to-all-done.9 = bf16[8,14,1536]{2,1,0:T(8,128)(2,1)S(1)} async-done(((bf16[8,14,1536]{2,1,0:T(8,128)(2,1)}), bf16[8,14,1536]{2,1,0:T(8,128)(2,1)S(1)}, u32[]{:S(2)}, u32[]{:S(2)}) %all-to-all-start.9) | async-done | bytes 344096 | tf_op jit(solution)/shard_map/all_to_all | solution.py:66
  436.7 5.5 %all-to-all-start.6 = ((bf16[64,64,1,96]{3,1,2,0:T(8,128)(2,1)}), bf16[64,64,1,96]{3,1,2,0:T(8,128)(2,1)S(1)}, u32[]{:S(2)}, u32[]{:S(2)}) async-start(bf16[64,64,1,96]{3,1,2,0:T(8,128)(2,1)} %bitcast.156), calls=%async_computation.6 | async-start | bytes 2097152 | tf_op jit(solution)/shard_map/all_to_all | solution.py:290
  443.4 25.3 %all-to-all-done.6 = bf16[64,64,1,96]{3,1,2,0:T(8,128)(2,1)S(1)} async-done(((bf16[64,64,1,96]{3,1,2,0:T(8,128)(2,1)}), bf16[64,64,1,96]{3,1,2,0:T(8,128)(2,1)S(1)}, u32[]{:S(2)}, u32[]{:S(2)}) %all-to-all-start.6) | async-done | bytes 786464 | tf_op jit(solution)/shard_map/all_to_all | solution.py:290
  469.3 4.0 all-to-all-start.10
  474.7 8.4 %all-to-all-done.10 = bf16[8,6,1536]{2,1,0:T(8,128)(2,1)} async-done(((bf16[8,6,1536]{2,1,0:T(8,128)(2,1)}), bf16[8,6,1536]{2,1,0:T(8,128)(2,1)}, u32[]{:S(2)}, u32[]{:S(2)}) %all-to-all-start.10) | async-done | bytes 147488 | tf_op jit(solution)/shard_map/all_to_all | solution.py:70
  483.1 4.9 all-to-all-start.7
  489.9 22.2 %all-to-all-done.7 = bf16[64,64,1,96]{3,1,2,0:T(8,128)(2,1)S(1)} async-done(((bf16[64,64,1,96]{3,1,2,0:T(8,128)(2,1)}), bf16[64,64,1,96]{3,1,2,0:T(8,128)(2,1)S(1)}, u32[]{:S(2)}, u32[]{:S(2)}) %all-to-all-start.7) | async-done | bytes 786464 | tf_op jit(solution)/shard_map/all_to_all | solution.py:293
  513.5 3.8 all-to-all-start.11
  527.0 2.2 all-to-all-done.11
  (304 shorter events, 102.4 us)
Async XLA Ops:
  7.2 40.8 %copy-start.9 = (bf16[64,2,1536]{2,1,0:T(2,128)(2,1)S(1)}, bf16[64,2,1536]{2,1,0:T(2,128)(2,1)}, u32[]{:S(2)}) copy-start(bf16[64,2,1536]{2,1,0:T(2,128)(2,1)} %param.16) | copy-start | bytes 1179652
  9.7 31.9 %all-to-all-start = ((bf16[64,32,1,96]{3,1,2,0:T(8,128)(2,1)}), bf16[64,32,1,96]{3,1,2,0:T(8,128)(2,1)}, u32[]{:S(2)}, u32[]{:S(2)}) async-start(bf16[64,32,1,96]{3,1,2,0:T(8,128)(2,1)} %bitcast.1), calls=%async_computation | async-start | bytes 1048576 | tf_op jit(solution)/shard_map/all_to_all | solution.py:212
  42.9 41.4 %copy-start.73 = (s32[2]{0:T(128)S(1)}, s32[2]{0:T(128)}, u32[]{:S(2)}) copy-start(s32[2]{0:T(128)} %param.17) | copy-start | bytes 28
  42.9 34.0 %all-to-all-start.1 = ((bf16[64,64,1,96]{3,1,2,0:T(8,128)(2,1)}), bf16[64,64,1,96]{3,1,2,0:T(8,128)(2,1)S(1)}, u32[]{:S(2)}, u32[]{:S(2)}) async-start(bf16[64,64,1,96]{3,1,2,0:T(8,128)(2,1)} %bitcast.5), calls=%async_computation.1 | async-start | bytes 2097152 | tf_op jit(solution)/shard_map/all_to_all | solution.py:216
  78.1 33.3 %all-to-all-start.2 = ((bf16[64,64,1,96]{3,1,2,0:T(8,128)(2,1)}), bf16[64,64,1,96]{3,1,2,0:T(8,128)(2,1)S(1)}, u32[]{:S(2)}, u32[]{:S(2)}) async-start(bf16[64,64,1,96]{3,1,2,0:T(8,128)(2,1)} %bitcast.152), calls=%async_computation.2 | async-start | bytes 2097152 | tf_op jit(solution)/shard_map/all_to_all | solution.py:217
  83.5 93.1 %all-gather.2.cloned.1.call-start = ((), (), s32[]{:S(2)}) async-start(), calls=%async_computation.12 | async-start | bytes 5898240 | tf_op jit(solution)/shard_map/all_gather | solution.py:232
  111.5 43.9 %copy-start.12 = (f32[31,1536]{1,0:T(8,128)S(1)}, f32[31,1536]{1,0:T(8,128)}, u32[]{:S(2)}) copy-start(f32[31,1536]{1,0:T(8,128)} %param.20) | copy-start | bytes 571396
  149.4 22.5 %all-to-all-start.3 = ((bf16[64,32,1,96]{3,1,2,0:T(8,128)(2,1)}), bf16[64,32,1,96]{3,1,2,0:T(8,128)(2,1)S(1)}, u32[]{:S(2)}, u32[]{:S(2)}) async-start(bf16[64,32,1,96]{3,1,2,0:T(8,128)(2,1)} %bitcast.14), calls=%async_computation.3 | async-start | bytes 1048576 | tf_op jit(solution)/shard_map/all_to_all | solution.py:226
  157.1 24.9 %copy-start.36 = (f32[64,2]{0,1:T(2,128)}, f32[64,2]{0,1:T(2,128)S(1)}, u32[]{:S(2)}) copy-start(f32[64,2]{0,1:T(2,128)S(1)} %compare_convert_fusion) | copy-start | bytes 1540
  175.0 5.2 copy-start.13
  182.0 15.4 %collective-permute-start = (bf16[15,2,1536]{2,0,1:T(8,128)(2,1)}, bf16[15,2,1536]{2,0,1:T(8,128)(2,1)S(1)}, u32[]{:S(2)}, u32[]{:S(2)}) collective-permute-start(bf16[15,2,1536]{2,0,1:T(8,128)(2,1)} %get-tuple-element.391), channel_id=1, source_target_pairs={{0,1},{1,2},{2,3},{3,4},{4,5},{5,6},{6,7},{7,8},{8,9},{9,10},{10,1... | collective-permute-start | bytes 276488 | tf_op jit(solution)/shard_map/ppermute | solution.py:22
  184.8 12.6 %collective-permute-start.1 = (bf16[15,2,1536]{2,0,1:T(8,128)(2,1)}, bf16[15,2,1536]{2,0,1:T(8,128)(2,1)S(1)}, u32[]{:S(2)}, u32[]{:S(2)}) collective-permute-start(bf16[15,2,1536]{2,0,1:T(8,128)(2,1)} %get-tuple-element.392), channel_id=1, source_target_pairs={{1,0},{2,1},{3,2},{4,3},{5,4},{6,5},{7,6},{8,7},{9,8},{10,9},{11,1... | collective-permute-start | bytes 276488 | tf_op jit(solution)/shard_map/ppermute | solution.py:23
  197.4 63.8 %collective-permute-start.4 = (bf16[128,768]{0,1:T(8,128)(2,1)}, bf16[128,768]{0,1:T(8,128)(2,1)}, u32[]{:S(2)}, u32[]{:S(2)}) collective-permute-start(bf16[128,768]{0,1:T(8,128)(2,1)} %bitcast.38), channel_id=1, source_target_pairs={{0,64},{64,0},{1,65},{65,1},{2,66},{66,2},{3,67},{67,3},{4,68},{68... | collective-permute-start | bytes 589832 | tf_op jit(solution)/shard_map/ppermute | solution.py:45
  205.7 30.4 %collective-permute-start.2 = (bf16[15,2,1536]{2,0,1:T(8,128)(2,1)S(1)}, bf16[15,2,1536]{2,0,1:T(8,128)(2,1)S(1)}, u32[]{:S(2)}, u32[]{:S(2)}) collective-permute-start(bf16[15,2,1536]{2,0,1:T(8,128)(2,1)S(1)} %get-tuple-element.389), channel_id=1, source_target_pairs={{0,1},{1,2},{2,3},{3,4},{4,5},{5,6},{6,7},{7,8},{8,9},{9,10},{10,1... | collective-permute-start | bytes 276488 | tf_op jit(solution)/shard_map/ppermute | solution.py:22
  207.6 28.7 %copy-start.14 = (f32[1536]{0:T(1024)S(1)}, f32[1536]{0:T(1024)}, u32[]{:S(2)}) copy-start(f32[1536]{0:T(1024)} %get-tuple-element.316) | copy-start | bytes 18436
  207.6 28.7 %copy-start.15 = (f32[1536]{0:T(1024)S(1)}, f32[1536]{0:T(1024)}, u32[]{:S(2)}) copy-start(f32[1536]{0:T(1024)} %get-tuple-element.317) | copy-start | bytes 18436
  207.6 28.7 %copy-start.16 = (f32[1536]{0:T(1024)S(1)}, f32[1536]{0:T(1024)}, u32[]{:S(2)}) copy-start(f32[1536]{0:T(1024)} %get-tuple-element.318) | copy-start | bytes 18436
  207.6 28.7 %copy-start.17 = (f32[1536]{0:T(1024)S(1)}, f32[1536]{0:T(1024)}, u32[]{:S(2)}) copy-start(f32[1536]{0:T(1024)} %get-tuple-element.319) | copy-start | bytes 18436
  207.6 28.7 %copy-start.18 = (f32[1536]{0:T(1024)S(1)}, f32[1536]{0:T(1024)}, u32[]{:S(2)}) copy-start(f32[1536]{0:T(1024)} %get-tuple-element.320) | copy-start | bytes 18436
  207.7 28.7 %copy-start.19 = (f32[1536]{0:T(1024)S(1)}, f32[1536]{0:T(1024)}, u32[]{:S(2)}) copy-start(f32[1536]{0:T(1024)} %get-tuple-element.321) | copy-start | bytes 18436
  207.7 28.7 %copy-start.20 = (f32[1536]{0:T(1024)S(1)}, f32[1536]{0:T(1024)}, u32[]{:S(2)}) copy-start(f32[1536]{0:T(1024)} %get-tuple-element.322) | copy-start | bytes 18436
  207.7 28.7 %copy-start.21 = (f32[1536]{0:T(1024)S(1)}, f32[1536]{0:T(1024)}, u32[]{:S(2)}) copy-start(f32[1536]{0:T(1024)} %get-tuple-element.323) | copy-start | bytes 18436
  207.7 28.7 %copy-start.22 = (f32[1536]{0:T(1024)S(1)}, f32[1536]{0:T(1024)}, u32[]{:S(2)}) copy-start(f32[1536]{0:T(1024)} %get-tuple-element.324) | copy-start | bytes 18436
  207.7 28.7 %copy-start.23 = (f32[1536]{0:T(1024)S(1)}, f32[1536]{0:T(1024)}, u32[]{:S(2)}) copy-start(f32[1536]{0:T(1024)} %get-tuple-element.325) | copy-start | bytes 18436
  207.7 28.7 %copy-start.24 = (f32[1536]{0:T(1024)S(1)}, f32[1536]{0:T(1024)}, u32[]{:S(2)}) copy-start(f32[1536]{0:T(1024)} %get-tuple-element.326) | copy-start | bytes 18436
  207.7 28.7 %copy-start.25 = (f32[1536]{0:T(1024)S(1)}, f32[1536]{0:T(1024)}, u32[]{:S(2)}) copy-start(f32[1536]{0:T(1024)} %get-tuple-element.327) | copy-start | bytes 18436
  207.7 28.7 %copy-start.26 = (f32[1536]{0:T(1024)S(1)}, f32[1536]{0:T(1024)}, u32[]{:S(2)}) copy-start(f32[1536]{0:T(1024)} %get-tuple-element.328) | copy-start | bytes 18436
  207.7 28.7 %copy-start.27 = (f32[1536]{0:T(1024)S(1)}, f32[1536]{0:T(1024)}, u32[]{:S(2)}) copy-start(f32[1536]{0:T(1024)} %get-tuple-element.329) | copy-start | bytes 18436
  207.7 28.7 %copy-start.28 = (f32[1536]{0:T(1024)S(1)}, f32[1536]{0:T(1024)}, u32[]{:S(2)}) copy-start(f32[1536]{0:T(1024)} %get-tuple-element.330) | copy-start | bytes 18436
  207.8 28.7 %copy-start.29 = (f32[1536]{0:T(1024)S(1)}, f32[1536]{0:T(1024)}, u32[]{:S(2)}) copy-start(f32[1536]{0:T(1024)} %get-tuple-element.331) | copy-start | bytes 18436
  207.8 28.7 %copy-start.30 = (f32[1536]{0:T(1024)S(1)}, f32[1536]{0:T(1024)}, u32[]{:S(2)}) copy-start(f32[1536]{0:T(1024)} %get-tuple-element.332) | copy-start | bytes 18436
  207.8 28.7 %copy-start.31 = (f32[1536]{0:T(1024)S(1)}, f32[1536]{0:T(1024)}, u32[]{:S(2)}) copy-start(f32[1536]{0:T(1024)} %get-tuple-element.333) | copy-start | bytes 18436
  207.8 28.7 %copy-start.32 = (f32[1536]{0:T(1024)S(1)}, f32[1536]{0:T(1024)}, u32[]{:S(2)}) copy-start(f32[1536]{0:T(1024)} %get-tuple-element.334) | copy-start | bytes 18436
  207.8 28.7 %copy-start.33 = (f32[1536]{0:T(1024)S(1)}, f32[1536]{0:T(1024)}, u32[]{:S(2)}) copy-start(f32[1536]{0:T(1024)} %get-tuple-element.335) | copy-start | bytes 18436
  207.8 28.7 %copy-start.34 = (f32[1536]{0:T(1024)S(1)}, f32[1536]{0:T(1024)}, u32[]{:S(2)}) copy-start(f32[1536]{0:T(1024)} %get-tuple-element.336) | copy-start | bytes 18436
  207.8 28.7 %copy-start.35 = (f32[1536]{0:T(1024)S(1)}, f32[1536]{0:T(1024)}, u32[]{:S(2)}) copy-start(f32[1536]{0:T(1024)} %get-tuple-element.337) | copy-start | bytes 18436
  207.8 28.7 %copy-start.37 = (f32[64,2]{0,1:T(2,128)S(1)}, f32[64,2]{0,1:T(2,128)}, u32[]{:S(2)}) copy-start(f32[64,2]{0,1:T(2,128)} %copy-done.36) | copy-start | bytes 1540
  207.8 28.7 %copy-start.39 = (f32[64,2]{0,1:T(2,128)S(1)}, f32[64,2]{0,1:T(2,128)}, u32[]{:S(2)}) copy-start(f32[64,2]{0,1:T(2,128)} %copy-done.38) | copy-start | bytes 1540
  207.8 28.7 %copy-start.72 = (f32[64,2]{0,1:T(2,128)S(1)}, f32[64,2]{0,1:T(2,128)}, u32[]{:S(2)}) copy-start(f32[64,2]{0,1:T(2,128)} %copy-done.71) | copy-start | bytes 1540
  207.9 28.3 %collective-permute-start.3 = (bf16[15,2,1536]{2,0,1:T(8,128)(2,1)S(1)}, bf16[15,2,1536]{2,0,1:T(8,128)(2,1)S(1)}, u32[]{:S(2)}, u32[]{:S(2)}) collective-permute-start(bf16[15,2,1536]{2,0,1:T(8,128)(2,1)S(1)} %get-tuple-element.390), channel_id=1, source_target_pairs={{1,0},{2,1},{3,2},{4,3},{5,4},{6,5},{7,6},{8,7},{9,8},{10,9},{11,1... | collective-permute-start | bytes 276488 | tf_op jit(solution)/shard_map/ppermute | solution.py:23
  236.5 5.6 %copy-start.8 = (bf16[64,2,1536]{2,1,0:T(2,128)(2,1)S(1)}, bf16[64,2,1536]{2,1,0:T(2,128)(2,1)}, u32[]{:S(2)}) copy-start(bf16[64,2,1536]{2,1,0:T(2,128)(2,1)} %param.21) | copy-start | bytes 1179652
  241.8 2.1 copy-start.42
  241.8 2.1 copy-start.43
  241.8 2.1 copy-start.44
  241.8 2.1 copy-start.45
  244.2 10.7 %copy-start.6 = (bf16[64,2,1536]{2,1,0:T(2,128)(2,1)}, bf16[64,2,1536]{2,1,0:T(2,128)(2,1)S(1)}, u32[]{:S(2)}) copy-start(bf16[64,2,1536]{2,1,0:T(2,128)(2,1)S(1)} %copy.191) | copy-start | bytes 1179652
  247.0 13.0 %collective-permute-start.6 = (f32[32,1536]{1,0:T(8,128)}, f32[32,1536]{1,0:T(8,128)}, u32[]{:S(2)}, u32[]{:S(2)}) collective-permute-start(f32[32,1536]{1,0:T(8,128)} %concatenate.34), channel_id=1, source_target_pairs={{0,64},{64,0},{1,65},{65,1},{2,66},{66,2},{3,67},{67,3},{4,68},{68... | collective-permute-start | bytes 589832 | tf_op jit(solution)/shard_map/ppermute | solution.py:47
  247.1 14.1 %collective-permute-start.5 = (bf16[128,1536]{1,0:T(8,128)(2,1)S(1)}, bf16[128,1536]{1,0:T(8,128)(2,1)}, u32[]{:S(2)}, u32[]{:S(2)}) collective-permute-start(bf16[128,1536]{1,0:T(8,128)(2,1)S(1)} %reshape.299), channel_id=1, source_target_pairs={{0,64},{64,0},{1,65},{65,1},{2,66},{66,2},{3,67},{67,3},{4,68},{68... | collective-permute-start | bytes 1179656 | tf_op jit(solution)/shard_map/ppermute | solution.py:46
  254.9 23.0 %all-to-all-start.4 = ((bf16[64,32,1,96]{3,1,2,0:T(8,128)(2,1)}), bf16[64,32,1,96]{3,1,2,0:T(8,128)(2,1)}, u32[]{:S(2)}, u32[]{:S(2)}) async-start(bf16[64,32,1,96]{3,1,2,0:T(8,128)(2,1)} %bitcast.162), calls=%async_computation.4 | async-start | bytes 1048576 | tf_op jit(solution)/shard_map/all_to_all | solution.py:281
  277.9 119.3 %all-to-all-start.8 = ((bf16[16,56,1536]{2,1,0:T(8,128)(2,1)}), bf16[16,56,1536]{2,1,0:T(8,128)(2,1)}, u32[]{:S(2)}, u32[]{:S(2)}) async-start(bf16[16,56,1536]{2,1,0:T(8,128)(2,1)} %pad_maximum_fusion), calls=%async_computation.8 | async-start | bytes 5505024 | tf_op jit(solution)/shard_map/all_to_all | solution.py:61
  288.0 5.9 %copy-start = (f32[512,4096]{1,0:T(8,128)}, f32[512,4096]{1,0:T(8,128)S(1)}, u32[]{:S(2)}) copy-start(f32[512,4096]{1,0:T(8,128)S(1)} %fusion.155) | copy-start | bytes 25165828 | tf_op jit(solution)/shard_map/while/body/eval_jaxpr/while
  315.1 5.9 %copy-start = (f32[512,4096]{1,0:T(8,128)}, f32[512,4096]{1,0:T(8,128)S(1)}, u32[]{:S(2)}) copy-start(f32[512,4096]{1,0:T(8,128)S(1)} %fusion.155) | copy-start | bytes 25165828 | tf_op jit(solution)/shard_map/while/body/eval_jaxpr/while
  343.3 5.9 %copy-start = (f32[512,4096]{1,0:T(8,128)}, f32[512,4096]{1,0:T(8,128)S(1)}, u32[]{:S(2)}) copy-start(f32[512,4096]{1,0:T(8,128)S(1)} %fusion.155) | copy-start | bytes 25165828 | tf_op jit(solution)/shard_map/while/body/eval_jaxpr/while
  371.5 5.9 %copy-start = (f32[512,4096]{1,0:T(8,128)}, f32[512,4096]{1,0:T(8,128)S(1)}, u32[]{:S(2)}) copy-start(f32[512,4096]{1,0:T(8,128)S(1)} %fusion.155) | copy-start | bytes 25165828 | tf_op jit(solution)/shard_map/while/body/eval_jaxpr/while
  397.2 24.3 %all-to-all-start.5 = ((bf16[64,32,1,96]{3,1,2,0:T(8,128)(2,1)}), bf16[64,32,1,96]{3,1,2,0:T(8,128)(2,1)S(1)}, u32[]{:S(2)}, u32[]{:S(2)}) async-start(bf16[64,32,1,96]{3,1,2,0:T(8,128)(2,1)} %bitcast.23), calls=%async_computation.5 | async-start | bytes 1048576 | tf_op jit(solution)/shard_map/all_to_all | solution.py:288
  406.2 67.2 %copy-start.1 = (f32[4096,96]{0,1:T(8,128)S(1)}, f32[4096,96]{0,1:T(8,128)}, u32[]{:S(2)}) copy-start(f32[4096,96]{0,1:T(8,128)} %get-tuple-element.155) | copy-start | bytes 4718596
  421.5 53.2 %copy-start.4 = (bf16[64,32,1,96]{3,1,2,0:T(8,128)(2,1)}, bf16[64,32,1,96]{3,1,2,0:T(8,128)(2,1)S(1)}, u32[]{:S(2)}) copy-start(bf16[64,32,1,96]{3,1,2,0:T(8,128)(2,1)S(1)} %all-to-all-done.5) | copy-start | bytes 1179652
  421.5 15.3 %all-to-all-start.9 = ((bf16[8,14,1536]{2,1,0:T(8,128)(2,1)}), bf16[8,14,1536]{2,1,0:T(8,128)(2,1)S(1)}, u32[]{:S(2)}, u32[]{:S(2)}) async-start(bf16[8,14,1536]{2,1,0:T(8,128)(2,1)} %pad_maximum_fusion.1), calls=%async_computation.9 | async-start | bytes 786432 | tf_op jit(solution)/shard_map/all_to_all | solution.py:66
  436.7 31.9 %all-to-all-start.6 = ((bf16[64,64,1,96]{3,1,2,0:T(8,128)(2,1)}), bf16[64,64,1,96]{3,1,2,0:T(8,128)(2,1)S(1)}, u32[]{:S(2)}, u32[]{:S(2)}) async-start(bf16[64,64,1,96]{3,1,2,0:T(8,128)(2,1)} %bitcast.156), calls=%async_computation.6 | async-start | bytes 2097152 | tf_op jit(solution)/shard_map/all_to_all | solution.py:290
  469.3 13.8 %all-to-all-start.10 = ((bf16[8,6,1536]{2,1,0:T(8,128)(2,1)}), bf16[8,6,1536]{2,1,0:T(8,128)(2,1)}, u32[]{:S(2)}, u32[]{:S(2)}) async-start(bf16[8,6,1536]{2,1,0:T(8,128)(2,1)} %broadcast_in_dim.115), calls=%async_computation.10 | async-start | bytes 393216 | tf_op jit(solution)/shard_map/all_to_all | solution.py:70
  474.7 42.7 %copy-start.7 = (bf16[64,2,1536]{2,0,1:T(8,128)(2,1)S(1)}, bf16[64,2,1536]{2,0,1:T(8,128)(2,1)}, u32[]{:S(2)}) copy-start(bf16[64,2,1536]{2,0,1:T(8,128)(2,1)} %get-tuple-element.384) | copy-start | bytes 1179652
  483.1 29.0 %all-to-all-start.7 = ((bf16[64,64,1,96]{3,1,2,0:T(8,128)(2,1)}), bf16[64,64,1,96]{3,1,2,0:T(8,128)(2,1)S(1)}, u32[]{:S(2)}, u32[]{:S(2)}) async-start(bf16[64,64,1,96]{3,1,2,0:T(8,128)(2,1)} %bitcast.155), calls=%async_computation.7 | async-start | bytes 2097152 | tf_op jit(solution)/shard_map/all_to_all | solution.py:293
  513.5 15.6 %all-to-all-start.11 = ((bf16[8,56,1536]{2,1,0:T(8,128)(2,1)}), bf16[8,56,1536]{2,1,0:T(8,128)(2,1)S(1)}, u32[]{:S(2)}, u32[]{:S(2)}) async-start(bf16[8,56,1536]{2,1,0:T(8,128)(2,1)} %broadcast_in_dim.116), calls=%async_computation.11 | async-start | bytes 2752512 | tf_op jit(solution)/shard_map/all_to_all | solution.py:72
  529.6 2.4 copy-start.11
  (33 other events, 63.7 us)
Sparse Core Ops, SparseCore 0:
  86.1 47.8 all-gather.1
